TPU v7x, 512 devices: a whole 4x8x8 slice. The times are simulated.
512 devices in a mesh: tm: 64 (over y_hi, x, z), rows: 8 (over y_lo, core).
Axes of the slice: x: 4, y: 8 (y_hi: 2, y_lo: 4; y = y_hi * 4 + y_lo), z: 8, core: 2. Of those that a mesh axis runs over, the one named last changes fastest.
Arguments:
- frames: bfloat16 [128, 16, 160, 256], P('tm', 'rows'), may hold values from -500 to 500
- norm_gain: float32 [256], replicated, may hold values from 0.1 to 1.9
- norm_shift: float32 [256], replicated, may hold values from -3 to 3
- conv_weight: bfloat16 [3, 3, 3, 256, 256], replicated, may hold values from -0.078125 to 0.078125
- conv_bias: float32 [256], replicated, may hold values from -3 to 3
Outputs:
- decoded: bfloat16 [128, 16, 160, 256], P('tm', 'rows')
All inputs are finite; a program needn't handle non-finite values.
Results may differ from a plain program's by a relative error of at most 0.0043.
Values may be sent and summed in bfloat16 or wider, within the bound.
A program may use at most 64 MiB of HBM per device.

v0:
```python
import jax
import jax.numpy as jnp
from jax import lax
from jax.sharding import PartitionSpec as P

GROUPS = 32


def from_behind(block, axis, distance):
    devices = range(lax.axis_size(axis))
    route = [(i - distance, i) for i in devices if i - distance in devices]
    return lax.ppermute(block, axis, route)


def with_halo(cells, sides, width):
    for axis, dim in sides:
        count = lax.axis_size(axis)
        ends = count - 1
        head = lax.slice_in_dim(cells, 0, width, axis=dim)
        tail = lax.slice_in_dim(cells, cells.shape[dim] - width, cells.shape[dim], axis=dim)
        cells = jnp.concatenate(
            [
                lax.ppermute(tail, axis, [(i, (i + 1) % count) for i in range(ends)]),
                cells,
                lax.ppermute(head, axis, [((i + 1) % count, i) for i in range(ends)]),
            ],
            axis=dim,
        )
    return cells


def pad_time(volume):
    earlier = from_behind(volume, "tm", 1)
    repeated = jnp.concatenate([volume[:1], volume[:1]], axis=0)
    earlier = jnp.where(lax.axis_index("tm") == 0, repeated, earlier)
    return jnp.concatenate([earlier, volume], axis=0)


def pad_rows(volume):
    extended = with_halo(volume, (("rows", 1),), 1)
    position = lax.axis_index("rows")
    final_index = lax.axis_size("rows") - 1
    upper_rim = jnp.where(position == 0, extended[:, 1:2], extended[:, 0:1])
    bottom = jnp.where(position == final_index, extended[:, -2:-1], extended[:, -1:])
    return jnp.concatenate([upper_rim, extended[:, 1:-1], bottom], axis=1)


def extend(volume):
    grown = pad_rows(pad_time(volume))
    return jnp.pad(grown, ((0, 0), (0, 0), (1, 1), (0, 0)), mode="edge")


def local(frames, norm_gain, norm_shift, conv_weight, conv_bias):
    frame_count, row_count, width_cells, channels = frames.shape
    group_width = channels // GROUPS
    cell_count = float(
        frame_count
        * row_count
        * width_cells
        * group_width
        * lax.axis_size("tm")
        * lax.axis_size("rows")
    )
    local_sum = jnp.sum(frames.reshape(-1, GROUPS, group_width), axis=(0, 2), dtype=jnp.float32)
    group_mean = lax.psum(local_sum, ("tm", "rows")) / cell_count
    mean_c = jnp.repeat(group_mean, group_width)
    centred = frames.astype(jnp.float32) - mean_c
    local_square = jnp.sum((centred * centred).reshape(-1, GROUPS, group_width), axis=(0, 2))
    group_var = lax.psum(local_square, ("tm", "rows")) / cell_count
    scale_c = jnp.repeat(lax.rsqrt(group_var + 1e-06), group_width)
    normed = (frames.astype(jnp.float32) - mean_c) * scale_c * norm_gain + norm_shift
    padded = extend(jax.nn.silu(normed).astype(jnp.bfloat16))
    running = jnp.zeros((frame_count * row_count * width_cells, channels), jnp.float32)
    for step_t in range(3):
        for step_y in range(3):
            window = padded[step_t : step_t + frame_count, step_y : step_y + row_count]
            columns = jnp.concatenate(
                [window[:, :, step_x : step_x + width_cells] for step_x in range(3)], axis=-1
            )
            kernel = conv_weight[step_t, step_y].reshape(3 * channels, channels)
            running = running + jnp.dot(
                columns.reshape(-1, 3 * channels), kernel, preferred_element_type=jnp.float32
            )
    return (
        (running + conv_bias)
        .reshape(frame_count, row_count, width_cells, channels)
        .astype(jnp.bfloat16)
    )


def solution(mesh):
    in_specs = (P("tm", "rows", None, None), P(), P(), P(), P())
    out_specs = P("tm", "rows", None, None)
    return jax.shard_map(local, mesh=mesh, in_specs=in_specs, out_specs=out_specs, check_vma=False)
```

profile of v0, /device:TPU:33, one launch (start us, length us, event | category | flops | bytes accessed | tf_op | source)
XLA Modules:
  0.0 252.2 jit_solution(11105472539908355193)
XLA Ops:
  0.0 1.1 convert_reduce_fusion
  1.3 102.6 %psum.14 = f32[32]{0:T(128)S(1)} all-reduce(f32[32]{0:T(128)S(1)} %reduce_sum.25), channel_id=1, replica_groups=mesh['tm'=64,'rows'=8] {'tm','rows'}, use_global_device_ids=true, to_apply=%region_2.0 | all-reduce | flops 32 | bytes 256 | tf_op jit(solution)/shard_map/psum | solution.py:65
  104.0 1.1 fusion.22
  105.3 94.4 %psum.15 = f32[32]{0:T(128)S(1)} all-reduce(f32[32]{0:T(128)S(1)} %reduce_sum.37), channel_id=1, replica_groups=mesh['tm'=64,'rows'=8] {'tm','rows'}, use_global_device_ids=true, to_apply=%region_5.6 | all-reduce | flops 32 | bytes 256 | tf_op jit(solution)/shard_map/psum | solution.py:69
  199.9 1.2 fusion.30
  201.1 3.1 %collective-permute-start = (bf16[2,2,160,256]{3,2,1,0:T(8,128)(2,1)S(1)}, bf16[2,2,160,256]{3,2,1,0:T(8,128)(2,1)S(1)}, u32[]{:S(2)}, u32[]{:S(2)}) collective-permute-start(bf16[2,2,160,256]{3,2,1,0:T(8,128)(2,1)S(1)} %fusion.30), channel_id=1, source_target_pairs={{0,8},{8,16},{16,24},{24,32},{32,40},{40,48},{48,56},{56,64},{64,7... | collective-permute-start | bytes 983048 | tf_op jit(solution)/shard_map/ppermute | solution.py:12
  204.2 15.5 %collective-permute-done = bf16[2,2,160,256]{3,2,1,0:T(8,128)(2,1)S(1)} collective-permute-done((bf16[2,2,160,256]{3,2,1,0:T(8,128)(2,1)S(1)}, bf16[2,2,160,256]{3,2,1,0:T(8,128)(2,1)S(1)}, u32[]{:S(2)}, u32[]{:S(2)}) %collective-permute-start) | collective-permute-done | bytes 327712 | tf_op jit(solution)/shard_map/ppermute | solution.py:12
  219.8 11.6 %collective-permute-start.1 = (bf16[4,1,160,256]{3,2,1,0:T(8,128)(2,1)S(1)}, bf16[4,1,160,256]{3,2,1,0:T(8,128)(2,1)S(1)}, u32[]{:S(2)}, u32[]{:S(2)}) collective-permute-start(bf16[4,1,160,256]{3,2,1,0:T(8,128)(2,1)S(1)} %fusion.31), channel_id=1, source_target_pairs={{0,1},{1,2},{2,3},{3,4},{4,5},{5,6},{6,7},{8,9},{9,10},{10,11},{11... | collective-permute-start | bytes 983048 | tf_op jit(solution)/shard_map/ppermute | solution.py:23
  231.4 4.0 %collective-permute-done.1 = bf16[4,1,160,256]{3,2,1,0:T(8,128)(2,1)S(1)} collective-permute-done((bf16[4,1,160,256]{3,2,1,0:T(8,128)(2,1)S(1)}, bf16[4,1,160,256]{3,2,1,0:T(8,128)(2,1)S(1)}, u32[]{:S(2)}, u32[]{:S(2)}) %collective-permute-start.1) | collective-permute-done | bytes 327712 | tf_op jit(solution)/shard_map/ppermute | solution.py:23
  235.4 1.9 collective-permute-start.2
  237.4 2.2 fusion.34
  239.6 5.0 %collective-permute-done.2 = bf16[4,1,160,256]{3,2,1,0:T(8,128)(2,1)S(1)} collective-permute-done((bf16[4,1,160,256]{3,2,1,0:T(8,128)(2,1)S(1)}, bf16[4,1,160,256]{3,2,1,0:T(8,128)(2,1)S(1)}, u32[]{:S(2)}, u32[]{:S(2)}) %collective-permute-start.2) | collective-permute-done | bytes 327712 | tf_op jit(solution)/shard_map/ppermute | solution.py:25
  244.8 0.6 fusion.8
  245.7 1.0 fusion.35
  246.7 0.4 fusion.39
  247.5 0.3 pad_maximum_fusion.14
  247.8 0.4 convolution_add_fusion.7
  248.2 0.4 convolution_add_fusion.6
  248.6 0.4 convolution_add_fusion.5
  249.1 0.4 convolution_add_fusion.4
  249.5 0.4 convolution_add_fusion.3
  250.0 0.4 convolution_add_fusion.2
  250.4 0.4 convolution_add_fusion.1
  251.1 1.2 fusion.17
  (25 shorter events, 1.9 us)
Async XLA Ops:
  201.1 18.6 %collective-permute-start = (bf16[2,2,160,256]{3,2,1,0:T(8,128)(2,1)S(1)}, bf16[2,2,160,256]{3,2,1,0:T(8,128)(2,1)S(1)}, u32[]{:S(2)}, u32[]{:S(2)}) collective-permute-start(bf16[2,2,160,256]{3,2,1,0:T(8,128)(2,1)S(1)} %fusion.30), channel_id=1, source_target_pairs={{0,8},{8,16},{16,24},{24,32},{32,40},{40,48},{48,56},{56,64},{64,7... | collective-permute-start | bytes 983048 | tf_op jit(solution)/shard_map/ppermute | solution.py:12
  219.8 15.6 %collective-permute-start.1 = (bf16[4,1,160,256]{3,2,1,0:T(8,128)(2,1)S(1)}, bf16[4,1,160,256]{3,2,1,0:T(8,128)(2,1)S(1)}, u32[]{:S(2)}, u32[]{:S(2)}) collective-permute-start(bf16[4,1,160,256]{3,2,1,0:T(8,128)(2,1)S(1)} %fusion.31), channel_id=1, source_target_pairs={{0,1},{1,2},{2,3},{3,4},{4,5},{5,6},{6,7},{8,9},{9,10},{10,11},{11... | collective-permute-start | bytes 983048 | tf_op jit(solution)/shard_map/ppermute | solution.py:23
  235.4 9.1 %collective-permute-start.2 = (bf16[4,1,160,256]{3,2,1,0:T(8,128)(2,1)S(1)}, bf16[4,1,160,256]{3,2,1,0:T(8,128)(2,1)S(1)}, u32[]{:S(2)}, u32[]{:S(2)}) collective-permute-start(bf16[4,1,160,256]{3,2,1,0:T(8,128)(2,1)S(1)} %get-tuple-element.6), channel_id=1, source_target_pairs={{1,0},{2,1},{3,2},{4,3},{5,4},{6,5},{7,6},{9,8},{10,9},{11,10},{12... | collective-permute-start | bytes 983048 | tf_op jit(solution)/shard_map/ppermute | solution.py:25
  250.4 0.7 copy-start
where the time goes:
time: 253 us; the launch traced here: 252 us
  blocking collectives  197 us (78%)
  waiting for transfers between devices  24.5 us (10%)
  starting transfers between devices  16.6 us (7%)
  other arithmetic  5.23 us (2%)
  matrix products  4.56 us (2%)
  local copies, waits for them, and re-layouts  4.12 us (2%)
    psum x1, blocking collectives, local(): group_mean = lax.psum(local_sum, ('tm', 'rows')) / cell_count  103 us
    psum x1, blocking collectives, local(): group_var = lax.psum(local_square, ('tm', 'rows')) / cell_count  94.4 us
    ppermute x1, waiting for transfers between devices, from_behind(): return lax.ppermute(block, axis, route)  15.5 us
    ppermute x1, starting transfers between devices, with_halo(): lax.ppermute(tail, axis, [(i, (i + 1) % count) for i in range(ends)])  11.6 us
  transfers between devices with their start and end apart: 3, of which 3 were waited for; matrix products, arithmetic and copies ran while one was open for 1% of the time, Pallas kernels for 0%

commit v1 on v0

v1 whole, which is shorter than its diff:
```python
import functools

import jax
import jax.numpy as jnp
from jax import lax
from jax.experimental import pallas as pl
from jax.experimental.pallas import tpu as pltpu
from jax.sharding import PartitionSpec as P

GROUPS = 32
MESH = pl.DeviceIdType.MESH
NX, NZ, NYLO, NCORE = 4, 8, 4, 2
NY = 8
TM, ROWS = 64, 8
STAGE_SIZES = (NX * NCORE, NZ, NY)


def position():
    t, r = lax.axis_index("tm"), lax.axis_index("rows")
    return (t // NZ) % NX, (t // (NX * NZ)) * NYLO + r // NCORE, t % NZ, r % NCORE


def device(x, y, z, core):
    return {"tm": (y // NYLO) * (NX * NZ) + x * NZ + z, "rows": (y % NYLO) * NCORE + core}


def stage_slot(stage):
    x, y, z, core = position()
    return (x * NCORE + core, z, y)[stage]


def stage_peer(stage, k):
    x, y, z, core = position()
    if stage == 0:
        other = (x * NCORE + core + k) % STAGE_SIZES[0]
        return device(other // NCORE, y, z, other % NCORE)
    if stage == 1:
        return device(x, y, (z + k) % NZ, core)
    return device(x, (y + k) % NY, z, core)


def remote(src, dst, send, recv, where):
    return pltpu.make_async_remote_copy(
        src_ref=src, dst_ref=dst, send_sem=send, recv_sem=recv, device_id=where, device_id_type=MESH
    )


def group_fold(v, group_width):
    lanes = v.shape[-1]
    lane = lax.broadcasted_iota(jnp.int32, v.shape, v.ndim - 1)
    step = 1
    while step < group_width:
        ahead = pltpu.roll(v, lanes - step, v.ndim - 1)
        behind = pltpu.roll(v, step, v.ndim - 1)
        v = v + jnp.where((lane // step) % 2 == 0, ahead, behind)
        step *= 2
    return v


def kernel(
    frames, gain, shift, weight, bias, out,
    raw, act, taps, acc, stats,
    own_sem, taps_sem, prev_send, prev_recv, row_send, row_recv, fwd_send, fwd_recv, stat_send, stat_recv,
):
    frame_count, row_count, width, channels = frames.shape
    group_width = channels // GROUPS
    cells = frame_count * row_count * width
    t, r = lax.axis_index("tm"), lax.axis_index("rows")
    has_prev, has_next = t > 0, t < TM - 1
    has_above, has_below = r > 0, r < ROWS - 1
    next_dev, prev_dev = {"tm": t + 1, "rows": r}, {"tm": t - 1, "rows": r}
    above_dev, below_dev = {"tm": t, "rows": r - 1}, {"tm": t, "rows": r + 1}

    barrier = pltpu.get_barrier_semaphore()
    peers = 0
    for stage, size in enumerate(STAGE_SIZES):
        for k in range(1, size):
            pl.semaphore_signal(barrier, inc=1, device_id=stage_peer(stage, k), device_id_type=MESH)
            peers += 1
    for there, where in ((has_prev, prev_dev), (has_above, above_dev), (has_below, below_dev)):

        @pl.when(there)
        def _():
            pl.semaphore_signal(barrier, inc=1, device_id=where, device_id_type=MESH)

    own_copy = pltpu.make_async_copy(frames, raw.at[2:4, 1:3], own_sem)
    own_copy.start()
    taps_copy = pltpu.make_async_copy(weight, taps, taps_sem)
    taps_copy.start()
    own_copy.wait()

    mine = raw[2:4, 1:3].reshape(cells, channels).astype(jnp.float32)
    count = float(cells * group_width)
    local_sum = jnp.sum(mine, axis=0, keepdims=True)
    local_mean = group_fold(local_sum, group_width) / count
    centred = mine - local_mean
    local_square = group_fold(jnp.sum(centred * centred, axis=0, keepdims=True), group_width)

    pl.semaphore_wait(
        barrier,
        peers + has_next.astype(jnp.int32) + has_above.astype(jnp.int32) + has_below.astype(jnp.int32),
    )

    def stage_start(stage, mean, square):
        slot = stage_slot(stage)
        stats[stage, slot] = jnp.concatenate([mean, square], axis=0)
        piece = stats.at[stage, slot]
        for k in range(1, STAGE_SIZES[stage]):
            remote(piece, piece, stat_send.at[stage], stat_recv.at[stage], stage_peer(stage, k)).start()

    def stage_finish(stage, n):
        size = STAGE_SIZES[stage]
        rest = stats.at[stage, pl.ds(0, size - 1)]
        pltpu.make_async_copy(rest, rest, stat_recv.at[stage]).wait()
        means, squares = stats[stage, :, 0:1, :], stats[stage, :, 1:2, :]
        mean = jnp.sum(means, axis=0) / size
        apart = means - mean[None]
        return mean, jnp.sum(squares, axis=0) + n * jnp.sum(apart * apart, axis=0), n * size

    stage_start(0, local_mean, local_square)

    prev_copies = [
        [
            remote(frames.at[f, y], raw.at[f, 1 + y], prev_send.at[f, y], prev_recv.at[f, y], next_dev)
            for y in range(2)
        ]
        for f in range(2)
    ]
    to_below = remote(frames.at[:, 1], raw.at[2:4, 0], row_send.at[0], row_recv.at[0], below_dev)
    to_above = remote(frames.at[:, 0], raw.at[2:4, 3], row_send.at[1], row_recv.at[1], above_dev)

    @pl.when(has_next)
    def _():
        for f in range(2):
            for y in range(2):
                prev_copies[f][y].start()

    @pl.when(has_below)
    def _():
        to_below.start()

    @pl.when(has_above)
    def _():
        to_above.start()

    mean, square, n = stage_finish(0, count)
    stage_start(1, mean, square)
    mean, square, n = stage_finish(1, n)
    stage_start(2, mean, square)

    pass_below = remote(raw.at[0:2, 2], raw.at[0:2, 0], fwd_send.at[0], fwd_recv.at[0], below_dev)
    pass_above = remote(raw.at[0:2, 1], raw.at[0:2, 3], fwd_send.at[1], fwd_recv.at[1], above_dev)

    def forward():
        for y, there, copy in ((0, has_above, pass_above), (1, has_below, pass_below)):
            for f in range(2):
                prev_copies[f][y].wait_recv()

            @pl.when(there)
            def _():
                copy.start()

    far = t == TM // 2

    @pl.when(has_prev & jnp.logical_not(far))
    def _():
        forward()

    mean, square, n = stage_finish(2, n)
    scale = lax.rsqrt(square / n + 1e-06) * gain[...]
    half_scale, half_shift = 0.5 * scale, 0.5 * shift[...]

    def activate(f, y, src_f, src_y):
        h = (raw[src_f, src_y].astype(jnp.float32) - mean) * half_scale + half_shift
        act[f, y] = (h + h * jnp.tanh(h)).astype(jnp.bfloat16)

    top = jnp.where(has_above, 0, 1)
    bottom = jnp.where(has_below, 3, 2)

    def window(a, frame_ids):
        parts = [act[frame_ids, b : b + 2] for b in range(3)]
        return jnp.concatenate([p.reshape(-1, channels) for p in parts], axis=-1)

    def tap(a, c):
        return jnp.concatenate([taps[a, b, c] for b in range(3)], axis=0)

    def dot(lhs, rhs):
        return jnp.dot(lhs, rhs, preferred_element_type=jnp.float32)

    for f in (2, 3):
        for y in (1, 2):
            activate(f, y, f, y)

    @pl.when(has_above)
    def _():
        to_below.wait_recv()

    @pl.when(has_below)
    def _():
        to_above.wait_recv()

    for f in (2, 3):
        activate(f, 0, f, top)
        activate(f, 3, f, bottom)
    taps_copy.wait()

    half = row_count * width
    both, late = window(2, slice(2, 4)), window(1, slice(2, 3))
    for c in range(3):
        acc[c] = dot(both, tap(2, c))
        acc[c, half:] += dot(late, tap(1, c))

    @pl.when(has_prev & far)
    def _():
        forward()

    src = [jnp.where(has_prev, f, 2) for f in range(2)]
    for f in range(2):
        for y in (1, 2):
            activate(f, y, src[f], y)

    @pl.when(has_prev & has_above)
    def _():
        pass_below.wait_recv()

    @pl.when(has_prev & has_below)
    def _():
        pass_above.wait_recv()

    for f in range(2):
        activate(f, 0, src[f], top)
        activate(f, 3, src[f], bottom)

    both, early = window(0, slice(0, 2)), window(1, slice(1, 2))
    for c in range(3):
        acc[c] += dot(both, tap(0, c))
        acc[c, :half] += dot(early, tap(1, c))

    column = lax.broadcasted_iota(jnp.int32, (width, channels), 0)
    for f in range(2):
        for y in range(2):
            rows = pl.ds((f * row_count + y) * width, width)
            left, right = acc[0, rows], acc[2, rows]
            left = jnp.where(column == 0, left, pltpu.roll(left, 1, 0))
            right = jnp.where(column == width - 1, right, pltpu.roll(right, width - 1, 0))
            out[f, y] = (left + acc[1, rows] + right + bias[...]).astype(jnp.bfloat16)

    @pl.when(has_next)
    def _():
        for f in range(2):
            for y in range(2):
                prev_copies[f][y].wait_send()

    @pl.when(has_below)
    def _():
        to_below.wait_send()

    @pl.when(has_above)
    def _():
        to_above.wait_send()

    @pl.when(has_prev & has_below)
    def _():
        pass_below.wait_send()

    @pl.when(has_prev & has_above)
    def _():
        pass_above.wait_send()

    for stage, size in enumerate(STAGE_SIZES):
        rest = stats.at[stage, pl.ds(0, size - 1)]
        pltpu.make_async_copy(rest, rest, stat_send.at[stage]).wait()


def local(frames, norm_gain, norm_shift, conv_weight, conv_bias):
    frame_count, row_count, width, channels = frames.shape
    vmem, anywhere = pl.BlockSpec(memory_space=pltpu.VMEM), pl.BlockSpec(memory_space=pl.ANY)
    dma = pltpu.SemaphoreType.DMA
    cells = frame_count * row_count * width
    return pl.pallas_call(
        kernel,
        out_shape=jax.ShapeDtypeStruct(frames.shape, jnp.bfloat16),
        in_specs=[anywhere, vmem, vmem, anywhere, vmem],
        out_specs=vmem,
        scratch_shapes=[
            pltpu.VMEM((4, 4, width, channels), jnp.bfloat16),
            pltpu.VMEM((4, 4, width, channels), jnp.bfloat16),
            pltpu.VMEM(conv_weight.shape, jnp.bfloat16),
            pltpu.VMEM((3, cells, channels), jnp.float32),
            pltpu.VMEM((3, 8, 2, channels), jnp.float32),
            dma, dma, dma((2, 2)), dma((2, 2)), dma((2,)), dma((2,)), dma((2,)), dma((2,)), dma((3,)), dma((3,)),
        ],
        compiler_params=pltpu.CompilerParams(
            collective_id=0, has_side_effects=True, vmem_limit_bytes=40 * 1024 * 1024
        ),
        name="norm_conv",
    )(
        frames,
        norm_gain.reshape(1, channels),
        norm_shift.reshape(1, channels),
        conv_weight,
        conv_bias.reshape(1, channels),
    )


def solution(mesh):
    in_specs = (P("tm", "rows", None, None), P(), P(), P(), P())
    out_specs = P("tm", "rows", None, None)
    return jax.shard_map(local, mesh=mesh, in_specs=in_specs, out_specs=out_specs, check_vma=False)
```

time: 253 us -> 44.1 us (0.17)
  the two profiles are of different devices: /device:TPU:33 before, /device:TPU:48 now
where the time goes in v1:
time: 44.1 us; the launch traced here: 43.8 us
  Pallas kernels  38.1 us (86%)
  local copies, waits for them, and re-layouts  5.73 us (13%)
    pallas_call x1, Pallas kernels, local(): pl.pallas_call(kernel, out_shape=jax.ShapeDtypeStruct(frames.shape, jnp.b...  38.1 us
    unnamed x11, local copies, waits for them, and re-layouts  5.73 us

profile of v1, /device:TPU:48, one launch (start us, length us, event | category | flops | bytes accessed | tf_op | source)
XLA Modules:
  0.0 43.8 jit_solution(17587647839262998856)
XLA Ops:
  0.0 0.0 copy-start
  0.0 2.0 %copy-done = bf16[3,3,3,256,256]{4,3,2,1,0:T(8,128)(2,1)S(1)} copy-done((bf16[3,3,3,256,256]{4,3,2,1,0:T(8,128)(2,1)S(1)}, bf16[3,3,3,256,256]{4,3,2,1,0:T(8,128)(2,1)}, u32[]{:S(2)}) %copy-start) | copy-done | bytes 3538968
  2.0 0.0 copy-start.1
  2.0 1.0 %copy-done.1 = bf16[2,2,160,256]{3,2,1,0:T(8,128)(2,1)S(1)} copy-done((bf16[2,2,160,256]{3,2,1,0:T(8,128)(2,1)S(1)}, bf16[2,2,160,256]{3,2,1,0:T(8,128)(2,1)}, u32[]{:S(2)}) %copy-start.1) | copy-done | bytes 327704
  3.0 0.0 copy-start.2
  3.0 0.7 %copy-done.2 = f32[256]{0:T(256)S(1)} copy-done((f32[256]{0:T(256)S(1)}, f32[256]{0:T(256)}, u32[]{:S(2)}) %copy-start.2) | copy-done | bytes 1048
  3.7 0.0 copy-start.3
  3.7 0.7 %copy-done.3 = f32[256]{0:T(256)S(1)} copy-done((f32[256]{0:T(256)S(1)}, f32[256]{0:T(256)}, u32[]{:S(2)}) %copy-start.3) | copy-done | bytes 1048
  4.3 0.0 copy-start.4
  4.3 0.7 %copy-done.4 = f32[256]{0:T(256)S(1)} copy-done((f32[256]{0:T(256)S(1)}, f32[256]{0:T(256)}, u32[]{:S(2)}) %copy-start.4) | copy-done | bytes 1048
  5.0 38.1 %norm_conv.1 = bf16[2,2,160,256]{3,2,1,0:T(8,128)(2,1)S(1)} custom-call(bf16[2,2,160,256]{3,2,1,0:T(8,128)(2,1)S(1)} %copy-done.1, f32[1,256]{1,0:T(1,128)S(1)} %bitcast.3, f32[1,256]{1,0:T(1,128)S(1)} %bitcast.4, bf16[3,3,3,256,256]{4,3,2,1,0:T(8,128)(2,1)S(1)} %copy-done, f32[1,256]{1,0:T(1,128)S(1)} %bitcast.5), custom_call_target="tpu_custom_call" | custom-call | tf_op jit(solution)/shard_map/norm_conv/pallas_call | solution.py:280
  43.1 0.7 %copy.7 = bf16[2,2,160,256]{3,2,1,0:T(8,128)(2,1)} copy(bf16[2,2,160,256]{3,2,1,0:T(8,128)(2,1)S(1)} %norm_conv.1) | data formatting | bytes 655360
Async XLA Ops:
  0.0 2.0 %copy-start = (bf16[3,3,3,256,256]{4,3,2,1,0:T(8,128)(2,1)S(1)}, bf16[3,3,3,256,256]{4,3,2,1,0:T(8,128)(2,1)}, u32[]{:S(2)}) copy-start(bf16[3,3,3,256,256]{4,3,2,1,0:T(8,128)(2,1)} %weight.1) | copy-start | bytes 10616836
  2.0 1.0 %copy-start.1 = (bf16[2,2,160,256]{3,2,1,0:T(8,128)(2,1)S(1)}, bf16[2,2,160,256]{3,2,1,0:T(8,128)(2,1)}, u32[]{:S(2)}) copy-start(bf16[2,2,160,256]{3,2,1,0:T(8,128)(2,1)} %frames.1) | copy-start | bytes 983044
  3.0 0.7 %copy-start.2 = (f32[256]{0:T(256)S(1)}, f32[256]{0:T(256)}, u32[]{:S(2)}) copy-start(f32[256]{0:T(256)} %param.6) | copy-start | bytes 3076
  3.7 0.7 %copy-start.3 = (f32[256]{0:T(256)S(1)}, f32[256]{0:T(256)}, u32[]{:S(2)}) copy-start(f32[256]{0:T(256)} %param.7) | copy-start | bytes 3076
  4.3 0.7 %copy-start.4 = (f32[256]{0:T(256)S(1)}, f32[256]{0:T(256)}, u32[]{:S(2)}) copy-start(f32[256]{0:T(256)} %param.9) | copy-start | bytes 3076

commit v2 on v1

--- a/solution.py
+++ b/solution.py
@@ -1,4 +1,5 @@
-import functools
+import itertools
+import math
 
 import jax
 import jax.numpy as jnp
@@ -9,34 +10,40 @@
 
 GROUPS = 32
 MESH = pl.DeviceIdType.MESH
-NX, NZ, NYLO, NCORE = 4, 8, 4, 2
-NY = 8
 TM, ROWS = 64, 8
-STAGE_SIZES = (NX * NCORE, NZ, NY)
-
-
-def position():
-    t, r = lax.axis_index("tm"), lax.axis_index("rows")
-    return (t // NZ) % NX, (t // (NX * NZ)) * NYLO + r // NCORE, t % NZ, r % NCORE
-
-
-def device(x, y, z, core):
-    return {"tm": (y // NYLO) * (NX * NZ) + x * NZ + z, "rows": (y % NYLO) * NCORE + core}
-
-
-def stage_slot(stage):
-    x, y, z, core = position()
-    return (x * NCORE + core, z, y)[stage]
-
-
-def stage_peer(stage, k):
-    x, y, z, core = position()
-    if stage == 0:
-        other = (x * NCORE + core + k) % STAGE_SIZES[0]
-        return device(other // NCORE, y, z, other % NCORE)
-    if stage == 1:
-        return device(x, y, (z + k) % NZ, core)
-    return device(x, (y + k) % NY, z, core)
+SIZE = {"x": 4, "y": 8, "z": 8, "core": 2}
+STAGES = (("z", "core"), ("x", "y"))
+SLOTS = max(math.prod(SIZE[a] for a in axes) for axes in STAGES)
+FAR = TM // 2
+RELAYS = (7, 24)
+
+
+def coordinates(t, r):
+    return {"x": (t >> 3) & 3, "y": ((t >> 5) << 2) + (r >> 1), "z": t & 7, "core": r & 1}
+
+
+def device(at):
+    y = at["y"]
+    return {"tm": ((y >> 2) << 5) + (at["x"] << 3) + at["z"], "rows": ((y & 3) << 1) + at["core"]}
+
+
+def stage_size(stage):
+    return math.prod(SIZE[a] for a in STAGES[stage])
+
+
+def stage_slot(stage, at):
+    slot = 0
+    for axis in STAGES[stage]:
+        slot = slot * SIZE[axis] + at[axis]
+    return slot
+
+
+def stage_peers(stage, at):
+    axes = STAGES[stage]
+    steps = list(itertools.product(*(range(SIZE[a]) for a in axes)))[1:]
+    hops = lambda step: sum(min(k, SIZE[a] - k) for a, k in zip(axes, step) if a != "core")
+    steps.sort(key=hops, reverse=True)
+    return [device(at | {a: (at[a] + k) & (SIZE[a] - 1) for a, k in zip(axes, step)}) for step in steps]
 
 
 def remote(src, dst, send, recv, where):
@@ -58,9 +65,9 @@
 
 
 def kernel(
-    frames, gain, shift, weight, bias, out,
-    raw, act, taps, acc, stats,
-    own_sem, taps_sem, prev_send, prev_recv, row_send, row_recv, fwd_send, fwd_recv, stat_send, stat_recv,
+    frames, gain_hbm, shift_hbm, weight, bias_hbm, out,
+    raw, act, taps, acc, relayed, stats, gain, shift, bias,
+    relay_send, relay_recv, vec_sem, own_sem, taps_sem, prev_send, prev_recv, row_send, row_recv, fwd_send, fwd_recv, stat_send, stat_recv,
 ):
     frame_count, row_count, width, channels = frames.shape
     group_width = channels // GROUPS
@@ -71,13 +78,18 @@
     next_dev, prev_dev = {"tm": t + 1, "rows": r}, {"tm": t - 1, "rows": r}
     above_dev, below_dev = {"tm": t, "rows": r - 1}, {"tm": t, "rows": r + 1}
 
+    at = coordinates(t, r)
+    peers = [stage_peers(stage, at) for stage in range(len(STAGES))]
+    far_sender, far = t == FAR - 1, t == FAR
+    is_relay = [t == place for place in RELAYS]
+    relay_devs = [{"tm": place, "rows": r} for place in RELAYS]
+    far_dev = {"tm": FAR, "rows": r}
+
     barrier = pltpu.get_barrier_semaphore()
-    peers = 0
-    for stage, size in enumerate(STAGE_SIZES):
-        for k in range(1, size):
-            pl.semaphore_signal(barrier, inc=1, device_id=stage_peer(stage, k), device_id_type=MESH)
-            peers += 1
-    for there, where in ((has_prev, prev_dev), (has_above, above_dev), (has_below, below_dev)):
+    for where in sum(peers, []):
+        pl.semaphore_signal(barrier, inc=1, device_id=where, device_id_type=MESH)
+    greeted = [(has_prev, prev_dev), (has_above, above_dev), (has_below, below_dev)]
+    for there, where in greeted + [(far, where) for where in relay_devs]:
 
         @pl.when(there)
         def _():
@@ -87,6 +99,12 @@
     own_copy.start()
     taps_copy = pltpu.make_async_copy(weight, taps, taps_sem)
     taps_copy.start()
+    vec_copies = [
+        pltpu.make_async_copy(src, dst, vec_sem.at[i])
+        for i, (src, dst) in enumerate(((gain_hbm, gain), (shift_hbm, shift), (bias_hbm, bias)))
+    ]
+    for copy in vec_copies:
+        copy.start()
     own_copy.wait()
 
     mine = raw[2:4, 1:3].reshape(cells, channels).astype(jnp.float32)
@@ -98,21 +116,22 @@
 
     pl.semaphore_wait(
         barrier,
-        peers + has_next.astype(jnp.int32) + has_above.astype(jnp.int32) + has_below.astype(jnp.int32),
+        len(sum(peers, []))
+        + sum(there.astype(jnp.int32) for there in [has_next, has_above, has_below, *is_relay]),
     )
 
     def stage_start(stage, mean, square):
-        slot = stage_slot(stage)
+        slot = stage_slot(stage, at)
         stats[stage, slot] = jnp.concatenate([mean, square], axis=0)
         piece = stats.at[stage, slot]
-        for k in range(1, STAGE_SIZES[stage]):
-            remote(piece, piece, stat_send.at[stage], stat_recv.at[stage], stage_peer(stage, k)).start()
+        for where in peers[stage]:
+            remote(piece, piece, stat_send.at[stage], stat_recv.at[stage], where).start()
 
     def stage_finish(stage, n):
-        size = STAGE_SIZES[stage]
+        size = stage_size(stage)
         rest = stats.at[stage, pl.ds(0, size - 1)]
         pltpu.make_async_copy(rest, rest, stat_recv.at[stage]).wait()
-        means, squares = stats[stage, :, 0:1, :], stats[stage, :, 1:2, :]
+        means, squares = stats[stage, 0:size, 0:1, :], stats[stage, 0:size, 1:2, :]
         mean = jnp.sum(means, axis=0) / size
         apart = means - mean[None]
         return mean, jnp.sum(squares, axis=0) + n * jnp.sum(apart * apart, axis=0), n * size
@@ -131,9 +150,18 @@
 
     @pl.when(has_next)
     def _():
-        for f in range(2):
-            for y in range(2):
-                prev_copies[f][y].start()
+        for y in range(2):
+            prev_copies[0][y].start()
+
+    @pl.when(has_next & jnp.logical_not(far_sender))
+    def _():
+        for y in range(2):
+            prev_copies[1][y].start()
+
+    @pl.when(far_sender)
+    def _():
+        for y in range(2):
+            remote(frames.at[1, y], relayed, prev_send.at[1, y], relay_recv, relay_devs[y]).start()
 
     @pl.when(has_below)
     def _():
@@ -145,8 +173,14 @@
 
     mean, square, n = stage_finish(0, count)
     stage_start(1, mean, square)
-    mean, square, n = stage_finish(1, n)
-    stage_start(2, mean, square)
+
+    relay_copies = [remote(relayed, raw.at[1, 1 + y], relay_send, prev_recv.at[1, y], far_dev) for y in range(2)]
+    for there, copy, where in zip(is_relay, relay_copies, relay_devs):
+
+        @pl.when(there)
+        def _():
+            remote(frames.at[1, 0], relayed, relay_send, relay_recv, where).wait_recv()
+            copy.start()
 
     pass_below = remote(raw.at[0:2, 2], raw.at[0:2, 0], fwd_send.at[0], fwd_recv.at[0], below_dev)
     pass_above = remote(raw.at[0:2, 1], raw.at[0:2, 3], fwd_send.at[1], fwd_recv.at[1], above_dev)
@@ -160,13 +194,13 @@
             def _():
                 copy.start()
 
-    far = t == TM // 2
-
     @pl.when(has_prev & jnp.logical_not(far))
     def _():
         forward()
 
-    mean, square, n = stage_finish(2, n)
+    for copy in vec_copies:
+        copy.wait()
+    mean, square, n = stage_finish(1, n)
     scale = lax.rsqrt(square / n + 1e-06) * gain[...]
     half_scale, half_shift = 0.5 * scale, 0.5 * shift[...]
 
@@ -267,39 +301,54 @@
     def _():
         pass_above.wait_send()
 
-    for stage, size in enumerate(STAGE_SIZES):
-        rest = stats.at[stage, pl.ds(0, size - 1)]
+    for there, copy in zip(is_relay, relay_copies):
+
+        @pl.when(there)
+        def _():
+            copy.wait_send()
+
+    for stage in range(len(STAGES)):
+        rest = stats.at[stage, pl.ds(0, stage_size(stage) - 1)]
         pltpu.make_async_copy(rest, rest, stat_send.at[stage]).wait()
 
 
 def local(frames, norm_gain, norm_shift, conv_weight, conv_bias):
     frame_count, row_count, width, channels = frames.shape
-    vmem, anywhere = pl.BlockSpec(memory_space=pltpu.VMEM), pl.BlockSpec(memory_space=pl.ANY)
+    hbm = pl.BlockSpec(memory_space=pltpu.HBM)
     dma = pltpu.SemaphoreType.DMA
     cells = frame_count * row_count * width
     return pl.pallas_call(
         kernel,
-        out_shape=jax.ShapeDtypeStruct(frames.shape, jnp.bfloat16),
-        in_specs=[anywhere, vmem, vmem, anywhere, vmem],
-        out_specs=vmem,
+        out_shape=pltpu.VMEM(frames.shape, jnp.bfloat16),
+        in_specs=[hbm] * 5,
+        out_specs=pl.BlockSpec(memory_space=pltpu.VMEM),
         scratch_shapes=[
             pltpu.VMEM((4, 4, width, channels), jnp.bfloat16),
             pltpu.VMEM((4, 4, width, channels), jnp.bfloat16),
             pltpu.VMEM(conv_weight.shape, jnp.bfloat16),
             pltpu.VMEM((3, cells, channels), jnp.float32),
-            pltpu.VMEM((3, 8, 2, channels), jnp.float32),
-            dma, dma, dma((2, 2)), dma((2, 2)), dma((2,)), dma((2,)), dma((2,)), dma((2,)), dma((3,)), dma((3,)),
+            pltpu.VMEM((width, channels), jnp.bfloat16),
+            pltpu.VMEM((len(STAGES), SLOTS, 2, channels), jnp.float32),
+            pltpu.VMEM((1, channels), jnp.float32),
+            pltpu.VMEM((1, channels), jnp.float32),
+            pltpu.VMEM((1, channels), jnp.float32),
+            dma, dma, dma((3,)), dma, dma, dma((2, 2)), dma((2, 2)), dma((2,)), dma((2,)), dma((2,)), dma((2,)), dma((len(STAGES),)), dma((len(STAGES),)),
         ],
         compiler_params=pltpu.CompilerParams(
             collective_id=0, has_side_effects=True, vmem_limit_bytes=40 * 1024 * 1024
         ),
         name="norm_conv",
     )(
-        frames,
-        norm_gain.reshape(1, channels),
-        norm_shift.reshape(1, channels),
-        conv_weight,
-        conv_bias.reshape(1, channels),
+        *(
+            pltpu.with_memory_space_constraint(x, pltpu.HBM)
+            for x in (
+                frames,
+                norm_gain.reshape(1, channels),
+                norm_shift.reshape(1, channels),
+                conv_weight,
+                conv_bias.reshape(1, channels),
+            )
+        )
     )
 
 

time: 44.1 us -> 34.2 us (0.78)
  local copies, waits for them, and re-layouts: 5.73 us -> 0.73 us
  Pallas kernels: 38.1 us -> 33.4 us
    unnamed x11 -> x1, local copies, waits for them, and re-layouts: 5.73 us -> 0.73 us
    pallas_call x1, Pallas kernels: 38.1 us -> 33.4 us  [local(): pl.pallas_call(kernel, out_shape=pltpu.VMEM(frames.shape, jnp.bfloat16),...]
where the time goes in v2:
time: 34.2 us; the launch traced here: 34.1 us
  Pallas kernels  33.4 us (98%)
  local copies, waits for them, and re-layouts  0.73 us (2%)
    pallas_call x1, Pallas kernels, local(): pl.pallas_call(kernel, out_shape=pltpu.VMEM(frames.shape, jnp.bfloat16),...  33.4 us
    unnamed x1, local copies, waits for them, and re-layouts  0.73 us

profile of v2, /device:TPU:48, one launch (start us, length us, event | category | flops | bytes accessed | tf_op | source)
XLA Modules:
  0.0 34.1 jit_solution(2160468845243469364)
XLA Ops:
  0.0 33.4 %norm_conv.1 = bf16[2,2,160,256]{3,2,1,0:T(8,128)(2,1)S(1)} custom-call(bf16[2,2,160,256]{3,2,1,0:T(8,128)(2,1)} %frames.1, f32[1,256]{1,0:T(1,128)} %bitcast.3, f32[1,256]{1,0:T(1,128)} %bitcast.4, bf16[3,3,3,256,256]{4,3,2,1,0:T(8,128)(2,1)} %weight.1, f32[1,256]{1,0:T(1,128)} %bitcast.5), custom_call_target="tpu_custom_call" | custom-call | tf_op jit(solution)/shard_map/norm_conv/pallas_call | solution.py:320
  33.4 0.7 %copy.7 = bf16[2,2,160,256]{3,2,1,0:T(8,128)(2,1)} copy(bf16[2,2,160,256]{3,2,1,0:T(8,128)(2,1)S(1)} %norm_conv.1) | data formatting | bytes 655360

commit v3 on v2

v3 whole, which is shorter than its diff:
```python
import jax
import jax.numpy as jnp
from jax import lax
from jax.experimental import pallas as pl
from jax.experimental.pallas import tpu as pltpu
from jax.sharding import PartitionSpec as P

GROUPS = 32
MESH = pl.DeviceIdType.MESH
TM, ROWS = 64, 8
SIZE = {"x": 4, "y": 8, "z": 8, "core": 2}
HUBS = (0, 1, 2)
MEMBERS = {0: (5, 6, 7), 2: (4, 3)}
LINE = SIZE["z"] * SIZE["core"]
PLANE = SIZE["x"] * SIZE["y"]
FAR = TM // 2
PIECES = ((0, 0), (0, 1), (1, 0), (1, 1))
RELAYS = {(0, 1): 7, (1, 0): 30, (1, 1): 23}


def coordinates(t, r):
    return {"x": (t >> 3) & 3, "y": ((t >> 5) << 2) + (r >> 1), "z": t & 7, "core": r & 1}


def device(at):
    y = at["y"]
    return {"tm": ((y >> 2) << 5) + (at["x"] << 3) + at["z"], "rows": ((y & 3) << 1) + at["core"]}


def plane_peers(at):
    nx, ny = SIZE["x"], SIZE["y"]
    steps = [(i, j) for i in range(nx) for j in range(ny)][1:]
    steps.sort(key=lambda step: min(step[0], nx - step[0]) + min(step[1], ny - step[1]), reverse=True)
    return [device(at | {"x": (at["x"] + i) & (nx - 1), "y": (at["y"] + j) & (ny - 1)}) for i, j in steps]


def signal(semaphore, where):
    pl.semaphore_signal(semaphore, inc=1, device_id=where, device_id_type=MESH)


def pack(mean, square):
    half = mean.shape[-1] // 2
    lane = lax.broadcasted_iota(jnp.int32, (1, half), 1) % 4
    upper = jnp.where(lane == 1, mean[:, half:], square[:, half:])
    lower = jnp.where(lane == 0, mean[:, :half], square[:, :half])
    return jnp.where(lane % 2 == 0, lower, upper)


def unpack(packed):
    lane = lax.broadcasted_iota(jnp.int32, packed.shape, 1) % 4
    rows = jnp.concatenate([jnp.where(lane == k, packed, 0.0) for k in range(4)], axis=0)
    rows = group_fold(rows, 4)
    return jnp.concatenate([rows[0:1], rows[1:2]], axis=1), jnp.concatenate([rows[2:3], rows[3:4]], axis=1)


def combine(parts, n):
    added = jnp.sum(parts, axis=0)
    mean = added / parts.shape[0]
    apart = parts - mean[None]
    spread = pltpu.roll(jnp.sum(apart * apart, axis=0), 2, 1)
    lane = lax.broadcasted_iota(jnp.int32, mean.shape, 1) % 4
    return jnp.where(lane < 2, mean, added + n * spread)


def remote(src, dst, send, recv, where):
    return pltpu.make_async_remote_copy(
        src_ref=src, dst_ref=dst, send_sem=send, recv_sem=recv, device_id=where, device_id_type=MESH
    )


def group_fold(v, group_width):
    lanes = v.shape[-1]
    lane = lax.broadcasted_iota(jnp.int32, v.shape, v.ndim - 1)
    step = 1
    while step < group_width:
        ahead = pltpu.roll(v, lanes - step, v.ndim - 1)
        behind = pltpu.roll(v, step, v.ndim - 1)
        v = v + jnp.where((lane // step) % 2 == 0, ahead, behind)
        step *= 2
    return v


def kernel(
    frames, gain_hbm, shift_hbm, weight, bias_hbm, out,
    raw, act, taps, acc, relayed, line, plane, total, gain, shift, bias,
    vec_sem, own_sem, taps_sem, line_send, line_recv, plane_send, plane_recv, total_send, total_recv, pair_send, prev_send, prev_recv, row_send, row_recv,
    fwd_send, fwd_recv, relay_send, relay_recv,
):
    frame_count, row_count, width, channels = frames.shape
    group_width = channels // GROUPS
    cells = frame_count * row_count * width
    t, r = lax.axis_index("tm"), lax.axis_index("rows")
    has_prev, has_next = t > 0, t < TM - 1
    core = r & 1
    outer, inner = core, 1 - core
    has_cross = (r > 0) & (r < ROWS - 1)
    next_dev, prev_dev = {"tm": t + 1, "rows": r}, {"tm": t - 1, "rows": r}
    cross_dev, partner_dev = {"tm": t, "rows": r + 2 * core - 1}, {"tm": t, "rows": r + 1 - 2 * core}
    outer_slot, inner_slot = 3 - 3 * core, 3 * core

    at = coordinates(t, r)
    is_hub = (at["z"] <= HUBS[-1]) & (core == 1)
    hubs = [(at["z"] == z) & (core == 1) for z in HUBS]
    hub_devs = [device(at | {"z": z, "core": 1}) for z in HUBS]
    peers = plane_peers(at)
    line_slot, plane_slot = 2 * at["z"] + core, SIZE["y"] * at["x"] + at["y"]
    far_sender, far = t == FAR - 1, t == FAR
    is_relay = {piece: t == place for piece, place in RELAYS.items()}
    relay_devs = {piece: {"tm": place, "rows": r} for piece, place in RELAYS.items()}
    far_dev = {"tm": FAR, "rows": r}

    own_copy = pltpu.make_async_copy(frames, raw.at[2:4, 1:3], own_sem)
    own_copy.start()

    barrier = pltpu.get_barrier_semaphore()

    @pl.when(is_hub)
    def _():
        for dz in (4, 3, 5, 2, 6, 1, 7, 0):
            for dk in range(0 if dz else 1, 2):
                signal(barrier, device(at | {"z": (at["z"] + dz) & 7, "core": (core + dk) & 1}))
        for where in peers:
            signal(barrier, where)

    for hub_z, others in MEMBERS.items():

        @pl.when((at["z"] >= min(others)) & (at["z"] <= max(others)))
        def _():
            signal(barrier, device(at | {"z": hub_z, "core": 1}))

    signal(barrier, partner_dev)
    greeted = [(has_prev, prev_dev), (has_cross, cross_dev)]
    greeted += [(far, where) for where in relay_devs.values()]
    greeted += [(there, {"tm": FAR - 1, "rows": r}) for there in is_relay.values()]
    for there, where in greeted:

        @pl.when(there)
        def _():
            signal(barrier, where)

    vec_copies = [
        pltpu.make_async_copy(src, dst, vec_sem.at[i])
        for i, (src, dst) in enumerate(((gain_hbm, gain), (shift_hbm, shift), (bias_hbm, bias)))
    ]
    for copy in vec_copies:
        copy.start()
    own_copy.wait()
    taps_copy = pltpu.make_async_copy(weight, taps, taps_sem)
    taps_copy.start()

    mine = raw[2:4, 1:3].reshape(cells, channels).astype(jnp.float32)
    count = float(cells * group_width)
    local_sum = jnp.sum(mine, axis=0, keepdims=True)
    local_mean = group_fold(local_sum, group_width) / count
    centred = mine - local_mean
    local_square = group_fold(jnp.sum(centred * centred, axis=0, keepdims=True), group_width)

    greetings = 1 + jnp.where(is_hub, len(peers) - 1, 0) + len(hubs) + len(RELAYS) * far_sender.astype(jnp.int32)
    for hub_z, others in MEMBERS.items():
        greetings += jnp.where((at["z"] == hub_z) & (core == 1), 2 * len(others), 0)
    for there in [has_next, has_cross, *is_relay.values()]:
        greetings += there.astype(jnp.int32)
    pl.semaphore_wait(barrier, greetings)

    mine_ref = line.at[line_slot]
    mine_ref[...] = pack(local_mean, local_square)
    to_hubs = [
        (jnp.logical_not(here), remote(mine_ref, mine_ref, line_send.at[k], line_recv, where))
        for k, (here, where) in enumerate(zip(hubs, hub_devs))
    ]
    for there, copy in to_hubs:

        @pl.when(there)
        def _():
            copy.start()

    prev, onward, relay_in, relay_out = {}, {}, {}, {}
    for kind, f in PIECES:
        y, slot, where = ((outer, outer_slot, cross_dev), (inner, inner_slot, partner_dev))[kind]
        src, dst = frames.at[f, y], raw.at[f, 1 + y]
        prev[kind, f] = remote(src, dst, prev_send.at[kind, f], prev_recv.at[kind, f], next_dev)
        onward[kind, f] = remote(dst, raw.at[f, slot], fwd_send.at[kind, f], fwd_recv.at[kind, f], where)
        if (kind, f) in RELAYS:
            relay_in[kind, f] = remote(src, relayed, prev_send.at[kind, f], relay_recv, relay_devs[kind, f])
            relay_out[kind, f] = remote(relayed, dst, relay_send, prev_recv.at[kind, f], far_dev)
    to_cross = remote(frames.at[:, outer], raw.at[2:4, outer_slot], row_send.at[0], row_recv.at[0], cross_dev)
    to_partner = remote(frames.at[:, inner], raw.at[2:4, inner_slot], row_send.at[1], row_recv.at[1], partner_dev)

    @pl.when(has_next)
    def _():
        prev[0, 0].start()

    @pl.when(has_next & jnp.logical_not(far_sender))
    def _():
        prev[0, 1].start()

    @pl.when(far_sender)
    def _():
        for copy in relay_in.values():
            copy.start()

    @pl.when(has_cross)
    def _():
        to_cross.start()

    to_partner.start()

    @pl.when(has_next & jnp.logical_not(far_sender))
    def _():
        for f in range(2):
            prev[0, f].wait_send()
        for f in range(2):
            prev[1, f].start()

    for piece, there in is_relay.items():

        @pl.when(there)
        def _():
            relay_in[piece].wait_recv()
            relay_out[piece].start()

    plane_ref = plane.at[plane_slot]
    to_peers = [remote(plane_ref, plane_ref, plane_send, plane_recv, where) for where in peers]
    to_members = {
        hub_z: [
            remote(total, total, total_send, total_recv, device(at | {"z": z, "core": k})) for z in others for k in (0, 1)
        ]
        for hub_z, others in MEMBERS.items()
    }
    total_to_partner = remote(total, total, pair_send, total_recv, partner_dev)
    line_rest, plane_rest = line.at[pl.ds(0, LINE - 1)], plane.at[pl.ds(0, PLANE - 1)]

    @pl.when(is_hub)
    def _():
        pltpu.make_async_copy(line_rest, line_rest, line_recv).wait()
        plane_ref[...] = combine(line[...], count)
        for copy in to_peers:
            copy.start()

    def pass_on(kind, f):
        prev[kind, f].wait_recv()
        if kind:
            onward[kind, f].start()
        else:

            @pl.when(has_cross)
            def _():
                onward[kind, f].start()

    @pl.when(has_prev & jnp.logical_not(far))
    def _():
        pass_on(0, 0)
        pass_on(0, 1)

    for copy in vec_copies:
        copy.wait()

    @pl.when(is_hub)
    def _():
        pltpu.make_async_copy(plane_rest, plane_rest, plane_recv).wait()
        total[...] = combine(plane[...], count * LINE)
        total_to_partner.start()

    for hub_z, copies in to_members.items():

        @pl.when(is_hub & (at["z"] == hub_z))
        def _():
            for copy in copies:
                copy.start()

    @pl.when(jnp.logical_not(is_hub))
    def _():
        total_to_partner.wait_recv()

    @pl.when(has_prev & jnp.logical_not(far))
    def _():
        pass_on(1, 0)
        pass_on(1, 1)

    @pl.when(far)
    def _():
        pass_on(0, 0)

    mean, square = unpack(total[...])
    scale = lax.rsqrt(square / (count * LINE * PLANE) + 1e-06) * gain[...]
    half_scale, half_shift = 0.5 * scale, 0.5 * shift[...]

    def activate(f, y, src_f, src_y):
        h = (raw[src_f, src_y].astype(jnp.float32) - mean) * half_scale + half_shift
        act[f, y] = (h + h * jnp.tanh(h)).astype(jnp.bfloat16)

    top = jnp.where(r > 0, 0, 1)
    bottom = jnp.where(r < ROWS - 1, 3, 2)

    def window(a, frame_ids):
        parts = [act[frame_ids, b : b + 2] for b in range(3)]
        return jnp.concatenate([p.reshape(-1, channels) for p in parts], axis=-1)

    def tap(a, c):
        return jnp.concatenate([taps[a, b, c] for b in range(3)], axis=0)

    def dot(lhs, rhs):
        return jnp.dot(lhs, rhs, preferred_element_type=jnp.float32)

    for f in (2, 3):
        for y in (1, 2):
            activate(f, y, f, y)

    to_partner.wait_recv()

    @pl.when(has_cross)
    def _():
        to_cross.wait_recv()

    for f in (2, 3):
        activate(f, 0, f, top)
        activate(f, 3, f, bottom)
    taps_copy.wait()

    both, late = window(2, slice(2, 4)), window(1, slice(2, 3))
    for c in range(3):
        acc[c] = dot(both, tap(2, c)).reshape(acc.shape[1:])
        acc[c, 1] += dot(late, tap(1, c)).reshape(acc.shape[2:])

    @pl.when(far)
    def _():
        for kind, f in PIECES[1:]:
            pass_on(kind, f)

    src = [jnp.where(has_prev, f, 2) for f in range(2)]
    for f in range(2):
        for y in (1, 2):
            activate(f, y, src[f], y)

    def add(c, y, rows, b):
        for a in range(2):
            lhs = act[a:2, rows]
            acc[c, 0 : 2 - a, y] += dot(lhs.reshape(-1, channels), taps[a, b, c]).reshape(lhs.shape)

    for c in range(3):
        add(c, slice(0, 2), slice(1, 3), 1)
        add(c, 1, 1, 0)
        add(c, 0, 2, 2)

    @pl.when(has_prev & has_cross)
    def _():
        for f in range(2):
            onward[0, f].wait_recv()

    @pl.when(has_prev)
    def _():
        for f in range(2):
            onward[1, f].wait_recv()

    for f in range(2):
        activate(f, 0, src[f], top)
        activate(f, 3, src[f], bottom)
    for c in range(3):
        add(c, 0, 0, 0)
        add(c, 1, 3, 2)

    column = lax.broadcasted_iota(jnp.int32, (width, channels), 0)
    for f in range(2):
        for y in range(2):
            left, right = acc[0, f, y], acc[2, f, y]
            left = jnp.where(column == 0, left, pltpu.roll(left, 1, 0))
            right = jnp.where(column == width - 1, right, pltpu.roll(right, width - 1, 0))
            out[f, y] = (left + acc[1, f, y] + right + bias[...]).astype(jnp.bfloat16)

    @pl.when(has_next)
    def _():
        for copy in (prev[1, 0], prev[1, 1]):
            copy.wait_send()

    @pl.when(far_sender)
    def _():
        for f in range(2):
            prev[0, f].wait_send()

    @pl.when(has_cross)
    def _():
        to_cross.wait_send()

    to_partner.wait_send()

    @pl.when(has_prev & has_cross)
    def _():
        for f in range(2):
            onward[0, f].wait_send()

    @pl.when(has_prev)
    def _():
        for f in range(2):
            onward[1, f].wait_send()

    for piece, there in is_relay.items():

        @pl.when(there)
        def _():
            relay_out[piece].wait_send()

    for there, copy in to_hubs:

        @pl.when(there)
        def _():
            copy.wait_send()

    @pl.when(is_hub)
    def _():
        pltpu.make_async_copy(plane_rest, plane_rest, plane_send).wait()
        total_to_partner.wait_send()

    for hub_z, copies in to_members.items():

        @pl.when(is_hub & (at["z"] == hub_z))
        def _():
            sent = plane.at[pl.ds(0, len(copies))]
            pltpu.make_async_copy(sent, sent, total_send).wait()


def local(frames, norm_gain, norm_shift, conv_weight, conv_bias):
    frame_count, row_count, width, channels = frames.shape
    hbm = pl.BlockSpec(memory_space=pltpu.HBM)
    dma = pltpu.SemaphoreType.DMA
    return pl.pallas_call(
        kernel,
        out_shape=pltpu.VMEM(frames.shape, jnp.bfloat16),
        in_specs=[hbm] * 5,
        out_specs=pl.BlockSpec(memory_space=pltpu.VMEM),
        scratch_shapes=[
            pltpu.VMEM((4, 4, width, channels), jnp.bfloat16),
            pltpu.VMEM((4, 4, width, channels), jnp.bfloat16),
            pltpu.VMEM(conv_weight.shape, jnp.bfloat16),
            pltpu.VMEM((3, frame_count, row_count, width, channels), jnp.float32),
            pltpu.VMEM((width, channels), jnp.bfloat16),
            pltpu.VMEM((LINE, 1, channels // 2), jnp.float32),
            pltpu.VMEM((PLANE, 1, channels // 2), jnp.float32),
            pltpu.VMEM((1, channels // 2), jnp.float32),
            pltpu.VMEM((1, channels), jnp.float32),
            pltpu.VMEM((1, channels), jnp.float32),
            pltpu.VMEM((1, channels), jnp.float32),
            dma((3,)), dma, dma, dma((len(HUBS),)), dma, dma, dma, dma, dma, dma,
            dma((2, 2)), dma((2, 2)), dma((2,)), dma((2,)), dma((2, 2)), dma((2, 2)), dma, dma,
        ],
        compiler_params=pltpu.CompilerParams(
            collective_id=0, has_side_effects=True, vmem_limit_bytes=40 * 1024 * 1024
        ),
        name="norm_conv",
    )(
        *(
            pltpu.with_memory_space_constraint(x, pltpu.HBM)
            for x in (
                frames,
                norm_gain.reshape(1, channels),
                norm_shift.reshape(1, channels),
                conv_weight,
                conv_bias.reshape(1, channels),
            )
        )
    )


def solution(mesh):
    in_specs = (P("tm", "rows", None, None), P(), P(), P(), P())
    out_specs = P("tm", "rows", None, None)
    return jax.shard_map(local, mesh=mesh, in_specs=in_specs, out_specs=out_specs, check_vma=False)
```

time: 34.2 us -> 28.2 us (0.82)
  the two profiles are of different devices: /device:TPU:48 before, /device:TPU:1 now
where the time goes in v3:
time: 28.2 us; the launch traced here: 28 us
  Pallas kernels  27.3 us (97%)
  local copies, waits for them, and re-layouts  0.73 us (3%)
    pallas_call x1, Pallas kernels, local(): pl.pallas_call(kernel, out_shape=pltpu.VMEM(frames.shape, jnp.bfloat16),...  27.3 us
    unnamed x1, local copies, waits for them, and re-layouts  0.73 us

profile of v3, /device:TPU:1, one launch (start us, length us, event | category | flops | bytes accessed | tf_op | source)
XLA Modules:
  0.0 28.0 jit_solution(5032091886476614354)
XLA Ops:
  0.0 27.3 %norm_conv.1 = bf16[2,2,160,256]{3,2,1,0:T(8,128)(2,1)S(1)} custom-call(bf16[2,2,160,256]{3,2,1,0:T(8,128)(2,1)} %frames.1, f32[1,256]{1,0:T(1,128)} %bitcast.3, f32[1,256]{1,0:T(1,128)} %bitcast.4, bf16[3,3,3,256,256]{4,3,2,1,0:T(8,128)(2,1)} %weight.1, f32[1,256]{1,0:T(1,128)} %bitcast.5), custom_call_target="tpu_custom_call" | custom-call | tf_op jit(solution)/shard_map/norm_conv/pallas_call | solution.py:425
  27.3 0.7 %copy.7 = bf16[2,2,160,256]{3,2,1,0:T(8,128)(2,1)} copy(bf16[2,2,160,256]{3,2,1,0:T(8,128)(2,1)S(1)} %norm_conv.1) | data formatting | bytes 655360

commit v4 on v3

--- a/solution.py
+++ b/solution.py
@@ -36,6 +36,19 @@
 
 def signal(semaphore, where):
     pl.semaphore_signal(semaphore, inc=1, device_id=where, device_id_type=MESH)
+
+
+def fold_channels(mean, square, n):
+    lanes = mean.shape[-1]
+    lane = lax.broadcasted_iota(jnp.int32, (2, lanes), 1)
+    both = jnp.concatenate([mean, square], axis=0)
+    for step in (1, 2, 4):
+        ahead, behind = pltpu.roll(both, lanes - step, 1), pltpu.roll(both, step, 1)
+        other = jnp.where((lane // step) % 2 == 0, ahead, behind)
+        apart = both[0:1] - other[0:1]
+        added = both + other
+        both = jnp.concatenate([0.5 * added[0:1], added[1:2] + (0.5 * n * step) * apart * apart], axis=0)
+    return both[0:1], both[1:2]
 
 
 def pack(mean, square):
@@ -110,17 +123,8 @@
     far_dev = {"tm": FAR, "rows": r}
 
     own_copy = pltpu.make_async_copy(frames, raw.at[2:4, 1:3], own_sem)
-    own_copy.start()
 
     barrier = pltpu.get_barrier_semaphore()
-
-    @pl.when(is_hub)
-    def _():
-        for dz in (4, 3, 5, 2, 6, 1, 7, 0):
-            for dk in range(0 if dz else 1, 2):
-                signal(barrier, device(at | {"z": (at["z"] + dz) & 7, "core": (core + dk) & 1}))
-        for where in peers:
-            signal(barrier, where)
 
     for hub_z, others in MEMBERS.items():
 
@@ -136,6 +140,16 @@
 
         @pl.when(there)
         def _():
+            signal(barrier, where)
+
+    own_copy.start()
+
+    @pl.when(is_hub)
+    def _():
+        for dz in (4, 3, 5, 2, 6, 1, 7, 0):
+            for dk in range(0 if dz else 1, 2):
+                signal(barrier, device(at | {"z": (at["z"] + dz) & 7, "core": (core + dk) & 1}))
+        for where in peers:
             signal(barrier, where)
 
     vec_copies = [
@@ -150,10 +164,9 @@
 
     mine = raw[2:4, 1:3].reshape(cells, channels).astype(jnp.float32)
     count = float(cells * group_width)
-    local_sum = jnp.sum(mine, axis=0, keepdims=True)
-    local_mean = group_fold(local_sum, group_width) / count
-    centred = mine - local_mean
-    local_square = group_fold(jnp.sum(centred * centred, axis=0, keepdims=True), group_width)
+    channel_mean = jnp.sum(mine, axis=0, keepdims=True) * (1.0 / cells)
+    centred = mine - channel_mean
+    local_mean, local_square = fold_channels(channel_mean, jnp.sum(centred * centred, axis=0, keepdims=True), cells)
 
     greetings = 1 + jnp.where(is_hub, len(peers) - 1, 0) + len(hubs) + len(RELAYS) * far_sender.astype(jnp.int32)
     for hub_z, others in MEMBERS.items():
@@ -205,13 +218,6 @@
 
     to_partner.start()
 
-    @pl.when(has_next & jnp.logical_not(far_sender))
-    def _():
-        for f in range(2):
-            prev[0, f].wait_send()
-        for f in range(2):
-            prev[1, f].start()
-
     for piece, there in is_relay.items():
 
         @pl.when(there)
@@ -236,6 +242,13 @@
         plane_ref[...] = combine(line[...], count)
         for copy in to_peers:
             copy.start()
+
+    @pl.when(has_next & jnp.logical_not(far_sender))
+    def _():
+        for f in range(2):
+            prev[0, f].wait_send()
+        for f in range(2):
+            prev[1, f].start()
 
     def pass_on(kind, f):
         prev[kind, f].wait_recv()

time: 28.2 us -> 28.1 us (level)
  no operation moved by 1% of the time
where the time goes in v4:
time: 28.1 us; the launch traced here: 28 us
  Pallas kernels  27.2 us (97%)
  local copies, waits for them, and re-layouts  0.73 us (3%)
    pallas_call x1, Pallas kernels, local(): pl.pallas_call(kernel, out_shape=pltpu.VMEM(frames.shape, jnp.bfloat16),...  27.2 us
    unnamed x1, local copies, waits for them, and re-layouts  0.73 us

profile of v4, /device:TPU:1, one launch (start us, length us, event | category | flops | bytes accessed | tf_op | source)
XLA Modules:
  0.0 28.0 jit_solution(6400369367552866410)
XLA Ops:
  0.0 27.2 %norm_conv.1 = bf16[2,2,160,256]{3,2,1,0:T(8,128)(2,1)S(1)} custom-call(bf16[2,2,160,256]{3,2,1,0:T(8,128)(2,1)} %frames.1, f32[1,256]{1,0:T(1,128)} %bitcast.3, f32[1,256]{1,0:T(1,128)} %bitcast.4, bf16[3,3,3,256,256]{4,3,2,1,0:T(8,128)(2,1)} %weight.1, f32[1,256]{1,0:T(1,128)} %bitcast.5), custom_call_target="tpu_custom_call" | custom-call | tf_op jit(solution)/shard_map/norm_conv/pallas_call | solution.py:438
  27.2 0.7 %copy.7 = bf16[2,2,160,256]{3,2,1,0:T(8,128)(2,1)} copy(bf16[2,2,160,256]{3,2,1,0:T(8,128)(2,1)S(1)} %norm_conv.1) | data formatting | bytes 655360

commit v5 on v4

--- a/solution.py
+++ b/solution.py
@@ -265,6 +265,13 @@
         pass_on(0, 0)
         pass_on(0, 1)
 
+    to_partner.wait_recv()
+
+    @pl.when(has_cross)
+    def _():
+        to_cross.wait_recv()
+
+    taps_copy.wait()
     for copy in vec_copies:
         copy.wait()
 
@@ -319,16 +326,9 @@
         for y in (1, 2):
             activate(f, y, f, y)
 
-    to_partner.wait_recv()
-
-    @pl.when(has_cross)
-    def _():
-        to_cross.wait_recv()
-
     for f in (2, 3):
         activate(f, 0, f, top)
         activate(f, 3, f, bottom)
-    taps_copy.wait()
 
     both, late = window(2, slice(2, 4)), window(1, slice(2, 3))
     for c in range(3):

time: 28.1 us -> 27.8 us (0.989)
  no operation moved by 1% of the time
where the time goes in v5:
time: 27.8 us; the launch traced here: 27.7 us
  Pallas kernels  27 us (97%)
  local copies, waits for them, and re-layouts  0.73 us (3%)
    pallas_call x1, Pallas kernels, local(): pl.pallas_call(kernel, out_shape=pltpu.VMEM(frames.shape, jnp.bfloat16),...  27 us
    unnamed x1, local copies, waits for them, and re-layouts  0.73 us

profile of v5, /device:TPU:1, one launch (start us, length us, event | category | flops | bytes accessed | tf_op | source)
XLA Modules:
  0.0 27.7 jit_solution(7695333674804579403)
XLA Ops:
  0.0 27.0 %norm_conv.1 = bf16[2,2,160,256]{3,2,1,0:T(8,128)(2,1)S(1)} custom-call(bf16[2,2,160,256]{3,2,1,0:T(8,128)(2,1)} %frames.1, f32[1,256]{1,0:T(1,128)} %bitcast.3, f32[1,256]{1,0:T(1,128)} %bitcast.4, bf16[3,3,3,256,256]{4,3,2,1,0:T(8,128)(2,1)} %weight.1, f32[1,256]{1,0:T(1,128)} %bitcast.5), custom_call_target="tpu_custom_call" | custom-call | tf_op jit(solution)/shard_map/norm_conv/pallas_call | solution.py:438
  27.0 0.7 %copy.7 = bf16[2,2,160,256]{3,2,1,0:T(8,128)(2,1)} copy(bf16[2,2,160,256]{3,2,1,0:T(8,128)(2,1)S(1)} %norm_conv.1) | data formatting | bytes 655360
